TPU v7x, 256 devices: a whole 4x4x8 slice. The times are simulated.
256 devices in a mesh: vocab: 8 (over x, z_lo), tok: 32 (over z_hi, y, core).
Axes of the slice: x: 4, y: 4, z: 8 (z_hi: 4, z_lo: 2; z = z_hi * 2 + z_lo), core: 2. Of those that a mesh axis runs over, the one named last changes fastest.
Arguments:
- hidden: bfloat16 [16384, 5376], P('tok', 'vocab'), may hold values from -2 to 2
- head_weight: bfloat16 [6144, 5376], P('vocab'), may hold values from -4 to 4
- targets: int32 [16384], P('tok'), may hold values from 0 to 6143
- loss_grad: float32 [16384], P('tok'), may hold values from 1 to 10
Outputs:
- input_grad: bfloat16 [16384, 5376], P('tok', 'vocab')
- head_grad: float32 [6144, 5376], P(('vocab', 'tok'))
- token_loss: float32 [16384], P('tok')
All inputs are finite; a program needn't handle non-finite values.
Results may differ from a plain program's by a relative error of at most 0.005.
Values may be sent and summed in bfloat16 or wider, within the bound.
A program may use at most 128 MiB of HBM per device.

v0:
```python
import jax
import jax.numpy as jnp
from jax import lax
from jax.sharding import PartitionSpec as P


def per_device(hidden, head_weight, targets, loss_grad):
    vocab_rows = head_weight.shape[0]
    portion = lax.all_gather(hidden, "vocab", axis=1, tiled=True)
    logits = lax.dot_general(
        portion, head_weight, (((1,), (1,)), ((), ())), preferred_element_type=jnp.float32
    )
    logits, full_hidden = (logits, portion)
    offset = lax.axis_index("vocab") * vocab_rows
    vocab_ids = offset + jnp.arange(vocab_rows, dtype=jnp.int32)
    matches = vocab_ids[None, :] == targets[:, None]
    target_part = jnp.sum(jnp.where(matches, logits, 0.0), axis=1)
    local_peak = jnp.max(logits, axis=1)
    row_peak = lax.pmax(local_peak, "vocab")
    local_total = jnp.sum(jnp.exp(logits - row_peak[:, None]), axis=1)
    row_total, target_logit = lax.psum((local_total, target_part), "vocab")
    log_total = row_peak + jnp.log(row_total)
    token_loss = log_total - target_logit
    probability = jnp.exp(logits - log_total[:, None])
    dlogits = (loss_grad[:, None] * (probability - matches.astype(jnp.float32))).astype(
        jnp.bfloat16
    )
    partial_grad = jnp.dot(dlogits, head_weight, preferred_element_type=jnp.float32)
    input_grad = lax.psum_scatter(partial_grad, "vocab", scatter_dimension=1, tiled=True).astype(
        jnp.bfloat16
    )
    head_grad = lax.psum_scatter(
        lax.dot_general(
            dlogits, full_hidden, (((0,), (0,)), ((), ())), preferred_element_type=jnp.float32
        ),
        "tok",
        scatter_dimension=0,
        tiled=True,
    )
    return (input_grad, head_grad, token_loss)


def solution(mesh):
    in_specs = (P("tok", "vocab"), P("vocab", None), P("tok"), P("tok"))
    out_specs = (P("tok", "vocab"), P(("vocab", "tok"), None), P("tok"))
    return jax.shard_map(
        per_device, mesh=mesh, in_specs=in_specs, out_specs=out_specs, check_vma=False
    )
```

profile of v0, /device:TPU:1, one launch (start us, length us, event | category | flops | bytes accessed | tf_op | source)
XLA Modules:
  0.0 585.7 jit_solution(18234469702458616286)
XLA Ops:
  7.2 0.0 all-gather.2.cloned.1.call-start
  7.2 0.7 all-gather.2.cloned.1.call-update
  7.9 0.0 reduce-scatter.3.cloned.1.call-start
  8.0 0.0 copy-start
  8.0 122.9 %all-gather.2.cloned.1.call-done = bf16[512,5376]{0,1:T(8,128)(2,1)} async-done(((bf16[512,672]{0,1:T(8,128)(2,1)}), bf16[512,5376]{0,1:T(8,128)(2,1)}) %all-gather.2.cloned.1.call-update) | async-done | bytes 5505040 | tf_op jit(solution)/shard_map/all_gather | solution.py:9
  130.8 8.9 %fusion.9 = (f32[512]{0:T(512)S(1)}, f32[512,768]{1,0:T(8,128)S(1)}) fusion(bf16[512,5376]{0,1:T(8,128)(2,1)} %all-gather.2.cloned.1.call-done, bf16[768,5376]{1,0:T(8,128)(2,1)} %param.5), kind=kOutput, calls=%fused_computation.12 | convolution fusion | flops 4228251136 | bytes 15337472 | tf_op jit(solution)/shard_map/dot_general | solution.py:10
  139.7 0.0 copy-start.1
  139.7 14.1 %pmax.7 = f32[512]{0:T(512)S(1)} all-reduce(f32[512]{0:T(512)S(1)} %get-tuple-element.9), channel_id=1, replica_groups=mesh['vocab'=8,'tok'=32] {'vocab'}, use_global_device_ids=true, to_apply=%region_1.2 | all-reduce | flops 512 | bytes 4096 | tf_op jit(solution)/shard_map/pmax | solution.py:19
  153.9 0.0 copy-done
  153.9 0.6 fusion.3
  154.5 12.6 %all-reduce = (f32[512]{0:T(512)S(1)}, f32[512]{0:T(512)S(1)}) all-reduce(f32[512]{0:T(512)S(1)} %get-tuple-element.4, f32[512]{0:T(512)S(1)} %get-tuple-element.3), channel_id=1, replica_groups=mesh['vocab'=8,'tok'=32] {'vocab'}, use_global_device_ids=true, to_apply=%region_3.4 | all-reduce | flops 1024 | bytes 8192 | tf_op jit(solution)/shard_map/psum | solution.py:21
  167.0 0.6 fusion.8
  167.6 0.0 copy-done.1
  167.6 12.9 %fusion.6 = f32[512,5376]{0,1:T(8,128)} fusion(bf16[768,5376]{1,0:T(8,128)(2,1)} %param.5, f32[512,768]{1,0:T(8,128)S(1)} %get-tuple-element.10, s32[768]{0:T(1024)S(1)} %iota_add_fusion, f32[512]{0:T(512)S(1)} %get-tuple-element.8, f32[512]{0:T(512)S(1)} %copy-done.1, s32[512]{0:T(512)S(1)} %copy-done), kind=kOutput, calls=%fused_computation.10 | convolution fusion | flops 4230217728 | bytes 20849664 | tf_op jit(solution)/shard_map/dot_general | solution.py:28
  180.5 0.0 reduce-scatter.3.cloned.1.call-update
  180.6 0.0 reduce-scatter.5.cloned.1.call-start
  180.6 11.0 %fusion.4 = f32[768,5376]{1,0:T(8,128)} fusion(bf16[512,5376]{0,1:T(8,128)(2,1)} %all-gather.2.cloned.1.call-done, f32[512,768]{1,0:T(8,128)S(1)} %get-tuple-element.10, s32[768]{0:T(1024)S(1)} %iota_add_fusion, f32[512]{0:T(512)S(1)} %get-tuple-element.8, f32[512]{0:T(512)S(1)} %copy-done.1, s32[512]{0:T(512)S(1)} %copy-done), kind=kOutput, calls=%fused_computation.9 | convolution fusion | flops 4230217728 | bytes 23602176 | tf_op jit(solution)/shard_map/dot_general | solution.py:33
  191.6 0.0 reduce-scatter.5.cloned.1.call-update
  191.7 217.3 %reduce-scatter.3.cloned.1.call-done = f32[512,672]{0,1:T(8,128)} async-done(((f32[512,5376]{0,1:T(8,128)}), f32[512,672]{0,1:T(8,128)}) %reduce-scatter.3.cloned.1.call-update) | async-done | bytes 1376272 | tf_op jit(solution)/shard_map/reduce_scatter | solution.py:29
  409.0 2.3 convert_element_type.11
  411.3 167.9 %reduce-scatter.5.cloned.1.call-done = f32[24,5376]{1,0:T(8,128)} async-done(((f32[768,5376]{1,0:T(8,128)}), f32[24,5376]{1,0:T(8,128)}) %reduce-scatter.5.cloned.1.call-update) | async-done | bytes 516112 | tf_op jit(solution)/shard_map/reduce_scatter | solution.py:32
  (1 shorter events, 0.0 us)
Async XLA Ops:
  7.2 123.7 %all-gather.2.cloned.1.call-start = ((), (), s32[]{:S(2)}) async-start(), calls=%async_computation.2 | async-start | bytes 6193152 | tf_op jit(solution)/shard_map/all_gather | solution.py:9
  7.9 401.1 %reduce-scatter.3.cloned.1.call-start = ((), (), s32[]{:S(2)}) async-start(), calls=%async_computation.3 | async-start | bytes 12386304 | tf_op jit(solution)/shard_map/reduce_scatter | solution.py:29
  8.0 145.9 %copy-start = (s32[512]{0:T(512)S(1)}, s32[512]{0:T(512)}, u32[]{:S(2)}) copy-start(s32[512]{0:T(512)} %param.6) | copy-start | bytes 6148
  139.7 27.9 %copy-start.1 = (f32[512]{0:T(512)S(1)}, f32[512]{0:T(512)}, u32[]{:S(2)}) copy-start(f32[512]{0:T(512)} %param.7) | copy-start | bytes 6148
  180.6 398.6 %reduce-scatter.5.cloned.1.call-start = ((), (), s32[]{:S(2)}) async-start(), calls=%async_computation.4 | async-start | bytes 17031168 | tf_op jit(solution)/shard_map/reduce_scatter | solution.py:32
Sparse Core Ops, SparseCore 0:
  9.8 120.9 all-gather.1
  180.7 228.2 reduce-scatter.2
  413.8 165.2 reduce-scatter.4
where the time goes:
time: 586 us
  waiting for transfers between devices  509 us (87%)
  matrix products  32.8 us (6%)
  blocking collectives  26.7 us (5%)
  between operations  13.8 us (2%)
    reduce_scatter x1, waiting for transfers between devices, per_device(): lax.psum_scatter(partial_grad, 'vocab', scatter_dimension=1, tiled=True)  217 us
    reduce_scatter x1, waiting for transfers between devices, per_device(): lax.psum_scatter(lax.dot_general(dlogits, full_hidden, (((0,), (0,)), (()...  168 us
    all_gather x1, waiting for transfers between devices, per_device(): portion = lax.all_gather(hidden, 'vocab', axis=1, tiled=True)  123 us
    pmax x1, blocking collectives, per_device(): row_peak = lax.pmax(local_peak, 'vocab')  14.1 us
    dot_general x1, matrix products, per_device(): jnp.dot(dlogits, head_weight, preferred_element_type=jnp.float32)  12.9 us
    psum x1, blocking collectives, per_device(): row_total, target_logit = lax.psum((local_total, target_part), 'vocab')  12.6 us
  transfers between devices with their start and end apart: 3, of which 3 were waited for; matrix products, arithmetic and copies ran while one was open for 2% of the time, Pallas kernels for 0%

commit v1 on v0

v1 whole, which is shorter than its diff:
```python
import jax
import jax.numpy as jnp
from jax import lax
from jax.experimental import pallas as pl
from jax.experimental.pallas import tpu as pltpu
from jax.sharding import PartitionSpec as P

MESH = pl.DeviceIdType.MESH
D = 5376
VOC = 768
TOK = 512
COL = 672
HALF = COL // 2
CUT = 560
CHUNKS = 3
WIDE = D // 2 // CHUNKS
GROUP = 48
BF = jnp.bfloat16
F32 = jnp.float32


def rows(start, size):
    return pl.ds(pl.multiple_of(start, 16), size)


def body(
    hidden, weight, targets, scales, grad_in, grad_head, loss,
    staged, weight_t, held, held_other, logits, dlog, dlog_other, stats,
    b_out, b_in, b_zout, b_zin, g_sum, c_out, c_in, c_zout, c_zin, last_out, last_in,
    local_sem, send_sem, recv_sem,
):
    vocab = lax.axis_index("vocab")
    tok = lax.axis_index("tok")
    x, z_lo = vocab // 2, vocab % 2
    core, y, z_hi = tok % 2, (tok // 2) % 4, tok // 8

    def in_vocab(dx, dz):
        return ((x + dx) % 4) * 2 + (z_lo + dz) % 2

    def in_tok(dz, dy, dc):
        return (((z_hi + dz) % 4) * 4 + (y + dy) % 4) * 2 + (core + dc) % 2

    def at_vocab(dx, dz):
        return (in_vocab(dx, dz), tok)

    def at_tok(dz, dy, dc):
        return (vocab, in_tok(dz, dy, dc))

    peers = [at_vocab(dx, dz) for dx in range(4) for dz in range(2) if dx or dz]
    others = [at_tok(0, 0, 1), at_tok(0, 1, 0), at_tok(0, 3, 0)]
    others += [at_tok(dz, 0, 0) for dz in (1, 2, 3)]

    barrier = pltpu.get_barrier_semaphore()
    for device in peers + others:
        pl.semaphore_signal(barrier, inc=1, device_id=device, device_id_type=MESH)

    fetch = pltpu.make_async_copy(weight, staged, local_sem)
    fetch.start()

    started = []

    def send(src, dst, device):
        at = len(started)
        copy = pltpu.make_async_remote_copy(
            src_ref=src,
            dst_ref=dst,
            send_sem=send_sem.at[at],
            recv_sem=recv_sem.at[at],
            device_id=device,
            device_id_type=MESH,
        )
        copy.start()
        started.append(copy)
        return copy

    def piece(block, start, stop):
        return held.at[rows(block * COL + start, stop - start)]

    def pass_on(block, start, stop, device):
        return send(piece(block, start, stop), piece(block, start, stop), device)

    right, left, pair = at_vocab(1, 0), at_vocab(3, 0), at_vocab(0, 1)
    own = vocab
    held[rows(own * COL, COL), :] = hidden[...].T
    pl.semaphore_wait(barrier, len(peers) + len(others))

    own_right_a = pass_on(own, 0, HALF, right)
    own_left_b = pass_on(own, HALF, COL, left)
    own_pair_a = pass_on(own, 0, HALF, pair)
    own_right_b = pass_on(own, HALF, COL, right)
    own_left_a = pass_on(own, 0, HALF, left)
    own_pair_b = pass_on(own, HALF, COL, pair)

    def turn(first, count):
        def step(i, _):
            at = pl.multiple_of((first + i) * 128, 128)
            weight_t[pl.ds(at, 128), :] = staged[:, pl.ds(at, 128)].T
            return 0

        lax.fori_loop(0, count, step, 0)

    def logit_part(block, fresh=False):
        def step(i, _):
            at = pl.multiple_of(i * 256, 256)
            part = lax.dot_general(
                weight_t[rows(block * COL, COL), pl.ds(at, 256)],
                held[rows(block * COL, COL), :],
                (((0,), (0,)), ((), ())),
                preferred_element_type=F32,
            )
            if fresh:
                logits[pl.ds(at, 256), :] = part
            else:
                logits[pl.ds(at, 256), :] += part
            return 0

        lax.fori_loop(0, VOC // 256, step, 0)

    fetch.wait()
    turn(0, 14)
    from_left, from_right = in_vocab(3, 0), in_vocab(1, 0)
    across, partner = in_vocab(2, 0), in_vocab(0, 1)
    own_right_a.wait_recv()
    on_right = pass_on(from_left, 0, HALF, right)
    own_left_b.wait_recv()
    on_left = pass_on(from_right, HALF, COL, left)
    turn(14, 14)
    own_pair_a.wait_recv()
    z_right_a = pass_on(partner, 0, HALF, right)
    z_left_a = pass_on(partner, 0, HALF, left)
    own_right_b.wait_recv()
    own_left_a.wait_recv()
    z_from_left = pass_on(from_left, CUT, COL, pair)
    z_from_right = pass_on(from_right, CUT, COL, pair)
    own_pair_b.wait_recv()
    z_right_b = pass_on(partner, HALF, CUT, right)
    z_left_b = pass_on(partner, HALF, CUT, left)
    turn(28, 14)
    on_right.wait_recv()
    z_across_a = pass_on(across, 0, HALF, pair)
    on_left.wait_recv()
    z_across_b = pass_on(across, HALF, COL, pair)
    logit_part(own, fresh=True)
    logit_part(from_left)
    logit_part(from_right)
    logit_part(partner)
    logit_part(across)
    z_from_left.wait_recv()
    z_right_a.wait_recv()
    z_right_b.wait_recv()
    logit_part(in_vocab(3, 1))
    z_from_right.wait_recv()
    z_left_a.wait_recv()
    z_left_b.wait_recv()
    logit_part(in_vocab(1, 1))
    z_across_a.wait_recv()
    z_across_b.wait_recv()
    share = send(
        held.at[rows((1 - core) * (D // 2), D // 2)], held_other, at_tok(0, 0, 1)
    )
    logit_part(in_vocab(2, 1))

    chosen = targets[...] - vocab * VOC
    steps = VOC // 64
    peak = jnp.full((8, TOK), -jnp.inf, F32)

    def find_peak(i, peak):
        part = logits[pl.ds(pl.multiple_of(i * 64, 64), 64), :]
        return jnp.maximum(peak, jnp.max(part.reshape(8, 8, TOK), axis=0))

    peak = lax.fori_loop(0, steps, find_peak, peak)
    peak = jnp.max(peak, axis=0, keepdims=True)
    ids = lax.broadcasted_iota(jnp.int32, (64, TOK), 0)

    def add_up(i, carry):
        total, picked = carry
        at = pl.multiple_of(i * 64, 64)
        part = logits[pl.ds(at, 64), :]
        hit = ids == chosen - at
        picked += jnp.sum(jnp.where(hit, part, 0.0).reshape(8, 8, TOK), axis=0)
        part = jnp.exp(part - peak)
        logits[pl.ds(at, 64), :] = part
        total += jnp.sum(part.reshape(8, 8, TOK), axis=0)
        return total, picked

    zeros = jnp.zeros((8, TOK), F32)
    total, picked = lax.fori_loop(0, steps, add_up, (zeros, zeros))
    total = jnp.sum(total, axis=0, keepdims=True)
    picked = jnp.sum(picked, axis=0, keepdims=True)
    stats[own] = jnp.concatenate([peak, total, picked, zeros[:5]], axis=0)
    told = [send(stats.at[own], stats.at[own], device) for device in peers]
    for copy in told:
        copy.wait_recv()
    heard = stats[...]
    peaks, totals, picks = heard[:, 0, :], heard[:, 1, :], heard[:, 2, :]
    row_peak = jnp.max(peaks, axis=0, keepdims=True)
    row_total = jnp.sum(totals * jnp.exp(peaks - row_peak), axis=0, keepdims=True)
    target_logit = jnp.sum(picks, axis=0, keepdims=True)
    loss[...] = row_peak + jnp.log(row_total) - target_logit
    share_of = jnp.exp(peak - row_peak) / row_total
    scale = scales[...]

    def make_dlog(i, _):
        at = pl.multiple_of(i * 64, 64)
        part = logits[pl.ds(at, 64), :] * share_of
        hit = ids == chosen - at
        part = scale * (part - jnp.where(hit, 1.0, 0.0))
        dlog[pl.ds(at, 64), :] = part.astype(BF)
        return 0

    lax.fori_loop(0, steps, make_dlog, 0)
    share_dlog = send(dlog, dlog_other, at_tok(0, 0, 1))

    def input_part(block, start):
        return jnp.dot(
            weight_t[rows(block * COL + start, HALF), :],
            dlog[...],
            preferred_element_type=F32,
        )

    def across_x(plane):
        block = in_vocab(2, plane)
        slots = b_out.at[plane], b_in.at[plane]
        slots[0][0] = input_part(block, 0).astype(BF)
        a = send(slots[0].at[0], slots[1].at[0], left)
        slots[0][1] = input_part(block, HALF).astype(BF)
        return a, send(slots[0].at[1], slots[1].at[1], right)

    def direct_x(plane):
        slots = b_out.at[plane], b_in.at[plane]
        slots[0][2] = input_part(in_vocab(3, plane), HALF).astype(BF)
        b = send(slots[0].at[2], slots[1].at[2], left)
        slots[0][3] = input_part(in_vocab(1, plane), 0).astype(BF)
        return b, send(slots[0].at[3], slots[1].at[3], right)

    def joined_x(plane, far):
        slots = b_out.at[plane], b_in.at[plane]
        far[0].wait_recv()
        part = input_part(in_vocab(3, plane), 0)
        slots[0][4] = (part + slots[1][0].astype(F32)).astype(BF)
        a = send(slots[0].at[4], slots[1].at[4], left)
        far[1].wait_recv()
        part = input_part(in_vocab(1, plane), HALF)
        slots[0][5] = (part + slots[1][1].astype(F32)).astype(BF)
        return a, send(slots[0].at[5], slots[1].at[5], right)

    def total_x(plane, near, joined):
        arrived = b_in.at[plane]
        block = in_vocab(0, plane)
        near[1].wait_recv()
        joined[0].wait_recv()
        a = input_part(block, 0) + arrived[3].astype(F32) + arrived[4].astype(F32)
        near[0].wait_recv()
        joined[1].wait_recv()
        b = input_part(block, HALF) + arrived[2].astype(F32) + arrived[5].astype(F32)
        return a, b

    up, down = at_tok(0, 1, 0), at_tok(0, 3, 0)

    def head_part(chunk):
        def step(i, _):
            two = pl.multiple_of(i * 384, 384)
            for mine, kept, first in (
                (dlog, held, core * (D // 2)),
                (dlog_other, held_other, 0),
            ):
                part = lax.dot_general(
                    mine[pl.ds(two, 384), :],
                    kept[rows(first + chunk * WIDE, WIDE), :],
                    (((1,), (1,)), ((), ())),
                    preferred_element_type=F32,
                ).reshape(2, 4, GROUP, WIDE)
                if kept is held:
                    g_sum[chunk, pl.ds(i * 2, 2)] = part
                else:
                    g_sum[chunk, pl.ds(i * 2, 2)] += part
            return 0

        lax.fori_loop(0, 2, step, 0)

    def far_y(chunk):
        to = (y + 2) % 4
        out, arrives = c_out.at[chunk], c_in.at[chunk]
        out[0] = g_sum[chunk, pl.ds(0, 2), to].astype(BF)
        a = send(out.at[0], arrives.at[0], down)
        out[1] = g_sum[chunk, pl.ds(2, 2), to].astype(BF)
        return a, send(out.at[1], arrives.at[1], up)

    def direct_y(chunk):
        out, arrives = c_out.at[chunk], c_in.at[chunk]
        out[2] = g_sum[chunk, pl.ds(2, 2), (y + 3) % 4].astype(BF)
        b = send(out.at[2], arrives.at[2], down)
        out[3] = g_sum[chunk, pl.ds(0, 2), (y + 1) % 4].astype(BF)
        return b, send(out.at[3], arrives.at[3], up)

    def joined_y(chunk, far):
        out, arrives = c_out.at[chunk], c_in.at[chunk]
        far[0].wait_recv()
        part = g_sum[chunk, pl.ds(0, 2), (y + 3) % 4]
        out[4] = (part + arrives[0].astype(F32)).astype(BF)
        a = send(out.at[4], arrives.at[4], down)
        far[1].wait_recv()
        part = g_sum[chunk, pl.ds(2, 2), (y + 1) % 4]
        out[5] = (part + arrives[1].astype(F32)).astype(BF)
        return a, send(out.at[5], arrives.at[5], up)

    def total_y(chunk, near, joined):
        arrives = c_in.at[chunk]
        near[1].wait_recv()
        joined[0].wait_recv()
        mine = g_sum.at[chunk, pl.ds(0, 2), y]
        mine[...] += arrives[3].astype(F32) + arrives[4].astype(F32)
        near[0].wait_recv()
        joined[1].wait_recv()
        mine = g_sum.at[chunk, pl.ds(2, 2), y]
        mine[...] += arrives[2].astype(F32) + arrives[5].astype(F32)
        copies = []
        for k in range(3):
            to = (z_hi + k + 1) % 4
            c_zout[chunk, k] = g_sum[chunk, to, y].astype(BF)
            copies.append(
                send(c_zout.at[chunk, k], c_zin.at[chunk, k], at_tok(k + 1, 0, 0))
            )
        return copies

    kept_rows = pl.ds(pl.multiple_of(core * 24, 8), 24)
    given_rows = pl.ds(pl.multiple_of((1 - core) * 24, 8), 24)

    def total_z(chunk, copies):
        for copy in copies:
            copy.wait_recv()
        mine = g_sum.at[chunk, z_hi, y]
        whole = mine[...]
        for k in range(3):
            whole += c_zin[chunk, k].astype(F32)
        mine[...] = whole
        last_out[chunk] = mine[given_rows, :]
        copy = send(last_out.at[chunk], last_in.at[chunk], at_tok(0, 0, 1))
        at = pl.multiple_of(core * (D // 2) + chunk * WIDE, 128)
        grad_head[:, pl.ds(at, WIDE)] = mine[kept_rows, :]
        return copy

    far_1 = across_x(1)
    share.wait_recv()
    share_dlog.wait_recv()
    head_part(0)
    far_c0, near_c0 = far_y(0), direct_y(0)
    near_1 = direct_x(1)
    head_part(1)
    far_c1, near_c1 = far_y(1), direct_y(1)
    far_0 = across_x(0)
    head_part(2)
    far_c2, near_c2 = far_y(2), direct_y(2)
    joined_c0 = joined_y(0, far_c0)
    joined_1 = joined_x(1, far_1)
    near_0 = direct_x(0)
    joined_c1 = joined_y(1, far_c1)
    joined_c2 = joined_y(2, far_c2)
    far_z0 = total_y(0, near_c0, joined_c0)
    a, b = total_x(1, near_1, joined_1)
    b_zout[0] = a.astype(BF)
    plane_a = send(b_zout.at[0], b_zin.at[0], pair)
    b_zout[1] = b.astype(BF)
    plane_b = send(b_zout.at[1], b_zin.at[1], pair)
    joined_0 = joined_x(0, far_0)
    far_z1 = total_y(1, near_c1, joined_c1)
    far_z2 = total_y(2, near_c2, joined_c2)
    last = [total_z(0, far_z0), total_z(1, far_z1)]
    a, b = total_x(0, near_0, joined_0)
    plane_a.wait_recv()
    plane_b.wait_recv()
    grad_in[:, pl.ds(0, HALF)] = (a + b_zin[0].astype(F32)).astype(BF).T
    grad_in[:, pl.ds(HALF, HALF)] = (b + b_zin[1].astype(F32)).astype(BF).T
    last.append(total_z(2, far_z2))
    for chunk in range(CHUNKS):
        last[chunk].wait_recv()
        at = pl.multiple_of((1 - core) * (D // 2) + chunk * WIDE, 128)
        grad_head[:, pl.ds(at, WIDE)] = last_in[chunk]
    for copy in started:
        copy.wait_send()


COPIES = 16 + 2 + 7 + 2 * 6 + 2 + CHUNKS * 10


def per_device(hidden, head_weight, targets, loss_grad):
    vmem = pl.BlockSpec(memory_space=pltpu.VMEM)
    grad_in, grad_head, loss = pl.pallas_call(
        body,
        out_shape=(
            jax.ShapeDtypeStruct((TOK, COL), BF),
            jax.ShapeDtypeStruct((24, D), F32),
            jax.ShapeDtypeStruct((1, TOK), F32),
        ),
        in_specs=[vmem, pl.BlockSpec(memory_space=pl.ANY), vmem, vmem],
        out_specs=(vmem, vmem, vmem),
        scratch_shapes=[
            pltpu.VMEM((VOC, D), BF),
            pltpu.VMEM((D, VOC), BF),
            pltpu.VMEM((D, TOK), BF),
            pltpu.VMEM((D // 2, TOK), BF),
            pltpu.VMEM((VOC, TOK), F32),
            pltpu.VMEM((VOC, TOK), BF),
            pltpu.VMEM((VOC, TOK), BF),
            pltpu.VMEM((8, 8, TOK), F32),
            pltpu.VMEM((2, 6, HALF, TOK), BF),
            pltpu.VMEM((2, 6, HALF, TOK), BF),
            pltpu.VMEM((2, HALF, TOK), BF),
            pltpu.VMEM((2, HALF, TOK), BF),
            pltpu.VMEM((CHUNKS, 4, 4, GROUP, WIDE), F32),
            pltpu.VMEM((CHUNKS, 6, 2, GROUP, WIDE), BF),
            pltpu.VMEM((CHUNKS, 6, 2, GROUP, WIDE), BF),
            pltpu.VMEM((CHUNKS, 3, GROUP, WIDE), BF),
            pltpu.VMEM((CHUNKS, 3, GROUP, WIDE), BF),
            pltpu.VMEM((CHUNKS, 24, WIDE), F32),
            pltpu.VMEM((CHUNKS, 24, WIDE), F32),
            pltpu.SemaphoreType.DMA,
            pltpu.SemaphoreType.DMA((COPIES,)),
            pltpu.SemaphoreType.DMA((COPIES,)),
        ],
        compiler_params=pltpu.CompilerParams(
            collective_id=0, has_side_effects=True, vmem_limit_bytes=62 * 2**20
        ),
        name="head_backward",
    )(hidden, head_weight, targets.reshape(1, TOK), loss_grad.reshape(1, TOK))
    return grad_in, grad_head, loss.reshape(TOK)


def solution(mesh):
    in_specs = (P("tok", "vocab"), P("vocab", None), P("tok"), P("tok"))
    out_specs = (P("tok", "vocab"), P(("vocab", "tok"), None), P("tok"))
    return jax.shard_map(
        per_device, mesh=mesh, in_specs=in_specs, out_specs=out_specs, check_vma=False
    )
```

time: 586 us -> 140 us (0.24)
  waiting for transfers between devices: 509 us -> 0 us
  Pallas kernels: 0 us -> 131 us
  matrix products: 32.8 us -> 0 us
  blocking collectives: 26.7 us -> 0 us
  between operations: 13.8 us -> 0.64 us
  local copies, waits for them, and re-layouts: 0.01 us -> 7.59 us
    reduce_scatter x2 -> x0, waiting for transfers between devices: 385 us -> none  [the longest x1 217 us: per_device(): lax.psum_scatter(partial_grad, 'vocab', scatter_dimension=1, tiled=True)]
    pallas_call x0 -> x1, Pallas kernels: none -> 131 us  [per_device(): pl.pallas_call(body, out_shape=(jax.ShapeDtypeStruct((TOK, COL), BF), jax...]
    all_gather x1 -> x0, waiting for transfers between devices: 123 us -> none  [per_device(): portion = lax.all_gather(hidden, 'vocab', axis=1, tiled=True)]
    dot_general x3 -> x0, matrix products: 32.8 us -> none  [the longest x1 12.9 us: per_device(): jnp.dot(dlogits, head_weight, preferred_element_type=jnp.float32)]
    pmax x1 -> x0, blocking collectives: 14.1 us -> none  [per_device(): row_peak = lax.pmax(local_peak, 'vocab')]
    psum x1 -> x0, blocking collectives: 12.6 us -> none  [per_device(): row_total, target_logit = lax.psum((local_total, target_part), 'vocab')]
    unnamed x4, local copies, waits for them, and re-layouts: 0.01 us -> 7.59 us
  transfers between devices with their start and end apart: 3 -> 0, of which waited for: 3 -> 0; matrix products, arithmetic and copies ran while one was open for 2% -> 0% of each run, Pallas kernels for 0% -> 0%
where the time goes in v1:
time: 140 us; the launch traced here: 139 us
  Pallas kernels  131 us (94%)
  local copies, waits for them, and re-layouts  7.59 us (5%)
    pallas_call x1, Pallas kernels, per_device(): pl.pallas_call(body, out_shape=(jax.ShapeDtypeStruct((TOK, COL), BF), jax...  131 us
    unnamed x4, local copies, waits for them, and re-layouts  7.59 us

profile of v1, /device:TPU:1, one launch (start us, length us, event | category | flops | bytes accessed | tf_op | source)
XLA Modules:
  0.0 139.4 jit_solution(3523326711398467850)
XLA Ops:
  0.6 2.3 %copy.7.hidden = bf16[512,672]{1,0:T(8,128)(2,1)} copy(bf16[512,672]{0,1:T(8,128)(2,1)} %param.4) | data formatting | bytes 1376256 | tf_op args[0]
  2.9 131.1 %head_backward.1 = (bf16[512,672]{1,0:T(8,128)(2,1)}, f32[24,5376]{1,0:T(8,128)}, f32[1,512]{1,0:T(1,128)}) custom-call(bf16[512,672]{1,0:T(8,128)(2,1)} %copy.7.hidden, bf16[768,5376]{1,0:T(8,128)(2,1)} %weight.1, s32[1,512]{1,0:T(1,128)} %bitcast.4, f32[1,512]{1,0:T(1,128)} %bitcast.5), custom_call_target="tpu_custom_call" | custom-call | tf_op jit(solution)/shard_map/head_backward/pallas_call | solution.py:388
  134.0 2.2 %copy.8 = bf16[512,672]{0,1:T(8,128)(2,1)} copy(bf16[512,672]{1,0:T(8,128)(2,1)} %get-tuple-element.9) | data formatting | bytes 1376256
  136.3 1.9 %copy.11 = f32[24,5376]{1,0:T(8,128)} copy(f32[24,5376]{1,0:T(8,128)} %get-tuple-element.16) | data formatting | bytes 1032192
  138.1 1.2 copy.12

commit v2 on v1

v2 whole, which is shorter than its diff:
```python
import jax
import jax.numpy as jnp
from jax import lax
from jax.experimental import pallas as pl
from jax.experimental.pallas import tpu as pltpu
from jax.sharding import PartitionSpec as P

MESH = pl.DeviceIdType.MESH
D = 5376
VOC = 768
TOK = 512
COL = 672
PIECE = 112
CHUNKS = 7
DEEP = 3
WIDE = D // 2 // CHUNKS
GROUP = 48
BF = jnp.bfloat16
F32 = jnp.float32


def rows(start, size):
    return pl.ds(pl.multiple_of(start, 16), size)


def body(
    hidden, weight, targets, scales, grad_in, grad_head, loss,
    staged, weight_t, held, held_other, logits, dlog, dlog_other, stats,
    b_out, b_in, b_zout, b_zin, g_sum, c_out, c_in, c_zout, c_zin, last_out, last_in,
    local_sem, send_sem, recv_sem,
):
    vocab = lax.axis_index("vocab")
    tok = lax.axis_index("tok")
    x, z_lo = vocab // 2, vocab % 2
    core, y, z_hi = tok % 2, (tok // 2) % 4, tok // 8

    def in_vocab(dx, dz):
        return ((x + dx) % 4) * 2 + (z_lo + dz) % 2

    def in_tok(dz, dy, dc):
        return (((z_hi + dz) % 4) * 4 + (y + dy) % 4) * 2 + (core + dc) % 2

    def at_vocab(dx, dz):
        return (in_vocab(dx, dz), tok)

    def at_tok(dz, dy, dc):
        return (vocab, in_tok(dz, dy, dc))

    peers = [at_vocab(dx, dz) for dx in range(4) for dz in range(2) if dx or dz]
    others = [at_tok(0, 0, 1), at_tok(0, 1, 0), at_tok(0, 3, 0)]
    others += [at_tok(dz, 0, 0) for dz in (1, 2, 3)]

    barrier = pltpu.get_barrier_semaphore()
    for device in peers + others:
        pl.semaphore_signal(barrier, inc=1, device_id=device, device_id_type=MESH)

    fetch_own = pltpu.make_async_copy(
        hidden, held.at[rows(vocab * COL, COL)], local_sem.at[0]
    )
    fetch_own.start()
    fetch = pltpu.make_async_copy(weight, staged, local_sem.at[1])
    fetch.start()

    started = []
    unsent = {}
    lanes = {}

    def send(src, dst, device, lane=None, most=2):
        at = len(started)
        copy = pltpu.make_async_remote_copy(
            src_ref=src,
            dst_ref=dst,
            send_sem=send_sem.at[at],
            recv_sem=recv_sem.at[at],
            device_id=device,
            device_id_type=MESH,
        )
        if lane is not None:
            queue = lanes.setdefault(lane, [])
            while len(queue) >= most:
                first = queue.pop(0)
                first.wait_send()
                del unsent[id(first)]
            queue.append(copy)
        copy.start()
        started.append(copy)
        unsent[id(copy)] = copy
        return copy

    right, left, pair = at_vocab(1, 0), at_vocab(3, 0), at_vocab(0, 1)
    own = vocab
    from_left, from_right = in_vocab(3, 0), in_vocab(1, 0)
    across, partner = in_vocab(2, 0), in_vocab(0, 1)

    arrival, ready = {}, set()

    def need(key, part):
        if (key, part) not in ready:
            ready.add((key, part))
            arrival[key, part].wait_recv()

    def pass_on(block, part, device, lane, key):
        where = held.at[rows(block * COL + part * PIECE, PIECE)]
        arrival[key, part] = send(where, where, device, lane)

    def own_right(part):
        pass_on(own, part, right, "right", "left")

    def own_left(part):
        pass_on(own, part, left, "left", "right")

    def own_pair(part):
        pass_on(own, part, pair, "pair", "pair")

    def on_right(part):
        need("left", part)
        pass_on(from_left, part, right, "right", "across")

    def on_left(part):
        need("right", part)
        pass_on(from_right, part, left, "left", "across")

    def z_right(part):
        need("pair", part)
        pass_on(partner, part, right, "right", "pair left")

    def z_left(part):
        need("pair", part)
        pass_on(partner, part, left, "left", "pair right")

    def pair_from_right(part):
        need("right", part)
        pass_on(from_right, part, pair, "pair", "pair right")

    def pair_from_left(part):
        need("left", part)
        pass_on(from_left, part, pair, "pair", "pair left")

    def pair_across(part):
        need("across", part)
        pass_on(across, part, pair, "pair", "pair across")

    fetch_own.wait()
    pl.semaphore_wait(barrier, len(peers) + len(others))

    def turn(first, count):
        def step(i, _):
            at = pl.multiple_of((first + i) * 128, 128)
            weight_t[pl.ds(at, 128), :] = staged[:, pl.ds(at, 128)].T
            return 0

        lax.fori_loop(0, count, step, 0)

    def logit_part(block, fresh=False):
        def step(i, _):
            at = pl.multiple_of(i * 256, 256)
            part = lax.dot_general(
                weight_t[rows(block * COL, COL), pl.ds(at, 256)],
                held[rows(block * COL, COL), :],
                (((0,), (0,)), ((), ())),
                preferred_element_type=F32,
            )
            if fresh:
                logits[pl.ds(at, 256), :] = part
            else:
                logits[pl.ds(at, 256), :] += part
            return 0

        lax.fori_loop(0, VOC // 256, step, 0)

    order_right = [(own_right, p) for p in (0, 1, 2)]
    order_right += [(on_right, 0), (own_right, 3), (on_right, 1), (own_right, 4)]
    order_right += [(on_right, 2), (own_right, 5)] + [(z_right, p) for p in range(5)]
    order_left = [(own_left, p) for p in (5, 4, 3)]
    order_left += [(on_left, 5), (own_left, 2), (on_left, 4), (own_left, 1)]
    order_left += [(on_left, 3), (own_left, 0)] + [(z_left, p) for p in range(5)]
    order_pair = [(own_pair, p) for p in range(6)]
    order_pair += [(pair_from_right, 5), (pair_across, 0), (pair_across, 5)]
    order_pair += [(pair_across, 1), (pair_across, 4), (pair_from_left, 5)]
    order_pair += [(pair_across, 2), (pair_across, 3)]
    def whole(key, block, fresh=False):
        for part in range(6):
            need(key, part)
        logit_part(block, fresh)

    for slot in range(14):
        for order in (order_right, order_left, order_pair):
            step, part = order[slot]
            step(part)
        if slot == 1:
            fetch.wait()
        if 1 <= slot <= 7:
            turn(6 * slot - 6, 6)
        if slot == 8:
            logit_part(own, fresh=True)
        if slot == 9:
            whole("pair", partner)
        if slot == 11:
            whole("left", from_left)
        if slot == 12:
            whole("right", from_right)
        if slot == 13:
            whole("across", across)
    whole("pair left", in_vocab(3, 1))
    whole("pair right", in_vocab(1, 1))
    for part in range(6):
        need("pair across", part)
    share = send(
        held.at[rows((1 - core) * (D // 2), D // 2)], held_other, at_tok(0, 0, 1)
    )
    logit_part(in_vocab(2, 1))

    chosen = targets[...] - vocab * VOC
    steps = VOC // 64
    peak = jnp.full((8, TOK), -jnp.inf, F32)

    def find_peak(i, peak):
        part = logits[pl.ds(pl.multiple_of(i * 64, 64), 64), :]
        return jnp.maximum(peak, jnp.max(part.reshape(8, 8, TOK), axis=0))

    peak = lax.fori_loop(0, steps, find_peak, peak)
    peak = jnp.max(peak, axis=0, keepdims=True)
    ids = lax.broadcasted_iota(jnp.int32, (64, TOK), 0)

    def add_up(i, carry):
        total, picked = carry
        at = pl.multiple_of(i * 64, 64)
        part = logits[pl.ds(at, 64), :]
        hit = ids == chosen - at
        picked += jnp.sum(jnp.where(hit, part, 0.0).reshape(8, 8, TOK), axis=0)
        part = jnp.exp(part - peak)
        logits[pl.ds(at, 64), :] = part
        total += jnp.sum(part.reshape(8, 8, TOK), axis=0)
        return total, picked

    zeros = jnp.zeros((8, TOK), F32)
    total, picked = lax.fori_loop(0, steps, add_up, (zeros, zeros))
    total = jnp.sum(total, axis=0, keepdims=True)
    picked = jnp.sum(picked, axis=0, keepdims=True)
    stats[own] = jnp.concatenate([peak, total, picked, zeros[:5]], axis=0)
    told = [send(stats.at[own], stats.at[own], device) for device in peers]
    for copy in told:
        copy.wait_recv()
    heard = stats[...]
    peaks, totals, picks = heard[:, 0, :], heard[:, 1, :], heard[:, 2, :]
    row_peak = jnp.max(peaks, axis=0, keepdims=True)
    row_total = jnp.sum(totals * jnp.exp(peaks - row_peak), axis=0, keepdims=True)
    target_logit = jnp.sum(picks, axis=0, keepdims=True)
    loss[...] = row_peak + jnp.log(row_total) - target_logit
    share_of = jnp.exp(peak - row_peak) / row_total
    scale = scales[...]

    def make_dlog(i, _):
        at = pl.multiple_of(i * 64, 64)
        part = logits[pl.ds(at, 64), :] * share_of
        hit = ids == chosen - at
        part = scale * (part - jnp.where(hit, 1.0, 0.0))
        dlog[pl.ds(at, 64), :] = part.astype(BF)
        return 0

    lax.fori_loop(0, steps, make_dlog, 0)
    share_dlog = send(dlog, dlog_other, at_tok(0, 0, 1))

    def input_part(block, part):
        return jnp.dot(
            weight_t[rows(block * COL + part * PIECE, PIECE), :],
            dlog[...],
            preferred_element_type=F32,
        )

    def to_left(group, slot, part):
        b_out[group, slot] = part.astype(BF)
        return send(
            b_out.at[group, slot], b_in.at[group, slot], left, "left", DEEP
        )

    def to_right(group, slot, part):
        b_out[group, slot] = part.astype(BF)
        return send(
            b_out.at[group, slot], b_in.at[group, slot], right, "right", DEEP
        )

    def arrived(group, slot):
        return b_in[group, slot].astype(F32)

    far_b, near_b, joined_b, plane_b = {}, {}, {}, {}

    def far_x(group):
        block, low = in_vocab(2, 1 - group // 3), group % 3
        a = to_left(group, 0, input_part(block, low))
        far_b[group] = a, to_right(group, 1, input_part(block, low + 3))

    def direct_x(group):
        plane, low = 1 - group // 3, group % 3
        b = to_left(group, 2, input_part(in_vocab(3, plane), low + 3))
        near_b[group] = b, to_right(group, 3, input_part(in_vocab(1, plane), low))

    def joined_x(group):
        plane, low = 1 - group // 3, group % 3
        part = input_part(in_vocab(3, plane), low)
        far_b[group][0].wait_recv()
        a = to_left(group, 4, part + arrived(group, 0))
        part = input_part(in_vocab(1, plane), low + 3)
        far_b[group][1].wait_recv()
        joined_b[group] = a, to_right(group, 5, part + arrived(group, 1))

    def total_x(group):
        plane, low = 1 - group // 3, group % 3
        block = in_vocab(0, plane)
        a, b = input_part(block, low), input_part(block, low + 3)
        near_b[group][1].wait_recv()
        joined_b[group][0].wait_recv()
        a += arrived(group, 3) + arrived(group, 4)
        near_b[group][0].wait_recv()
        joined_b[group][1].wait_recv()
        b += arrived(group, 2) + arrived(group, 5)
        if plane:
            b_zout[low] = a.astype(BF)
            a = send(b_zout.at[low], b_zin.at[low], pair)
            b_zout[low + 3] = b.astype(BF)
            plane_b[low] = a, send(b_zout.at[low + 3], b_zin.at[low + 3], pair)
        else:
            plane_b[low][0].wait_recv()
            a += b_zin[low].astype(F32)
            grad_in[pl.ds(low * PIECE, PIECE), :] = a.astype(BF)
            plane_b[low][1].wait_recv()
            b += b_zin[low + 3].astype(F32)
            grad_in[pl.ds((low + 3) * PIECE, PIECE), :] = b.astype(BF)

    up, down = at_tok(0, 1, 0), at_tok(0, 3, 0)

    def head_part(chunk):
        def step(i, _):
            two = pl.multiple_of(i * 384, 384)
            for mine, kept, first in (
                (dlog, held, core * (D // 2)),
                (dlog_other, held_other, 0),
            ):
                part = lax.dot_general(
                    mine[pl.ds(two, 384), :],
                    kept[rows(first + chunk * WIDE, WIDE), :],
                    (((1,), (1,)), ((), ())),
                    preferred_element_type=F32,
                ).reshape(2, 4, GROUP, WIDE)
                if kept is held:
                    g_sum[chunk, pl.ds(i * 2, 2)] = part
                else:
                    g_sum[chunk, pl.ds(i * 2, 2)] += part
            return 0

        lax.fori_loop(0, 2, step, 0)

    def to_down(chunk, slot, part):
        c_out[chunk, slot] = part.astype(BF)
        return send(
            c_out.at[chunk, slot], c_in.at[chunk, slot], down, "down", DEEP
        )

    def to_up(chunk, slot, part):
        c_out[chunk, slot] = part.astype(BF)
        return send(c_out.at[chunk, slot], c_in.at[chunk, slot], up, "up", DEEP)

    def landed(chunk, slot):
        return c_in[chunk, slot].astype(F32)

    far_c, near_c, joined_c, zs_c, last = {}, {}, {}, {}, {}
    low, high = pl.ds(0, 2), pl.ds(2, 2)

    def far_y(chunk):
        head_part(chunk)
        to = (y + 2) % 4
        a = to_down(chunk, 0, g_sum[chunk, low, to])
        far_c[chunk] = a, to_up(chunk, 1, g_sum[chunk, high, to])

    def direct_y(chunk):
        b = to_down(chunk, 2, g_sum[chunk, high, (y + 3) % 4])
        near_c[chunk] = b, to_up(chunk, 3, g_sum[chunk, low, (y + 1) % 4])

    def joined_y(chunk):
        far_c[chunk][0].wait_recv()
        a = to_down(chunk, 4, g_sum[chunk, low, (y + 3) % 4] + landed(chunk, 0))
        far_c[chunk][1].wait_recv()
        b = to_up(chunk, 5, g_sum[chunk, high, (y + 1) % 4] + landed(chunk, 1))
        joined_c[chunk] = a, b

    def total_y(chunk):
        near_c[chunk][1].wait_recv()
        joined_c[chunk][0].wait_recv()
        g_sum[chunk, low, y] += landed(chunk, 3) + landed(chunk, 4)
        near_c[chunk][0].wait_recv()
        joined_c[chunk][1].wait_recv()
        g_sum[chunk, high, y] += landed(chunk, 2) + landed(chunk, 5)
        copies = []
        for k in range(3):
            to = (z_hi + k + 1) % 4
            c_zout[chunk, k] = g_sum[chunk, to, y].astype(BF)
            copies.append(
                send(c_zout.at[chunk, k], c_zin.at[chunk, k], at_tok(k + 1, 0, 0))
            )
        zs_c[chunk] = copies

    kept_rows = pl.ds(pl.multiple_of(core * 24, 8), 24)
    given_rows = pl.ds(pl.multiple_of((1 - core) * 24, 8), 24)

    def total_z(chunk):
        for copy in zs_c[chunk]:
            copy.wait_recv()
        mine = g_sum.at[chunk, z_hi, y]
        total = mine[...]
        for k in range(3):
            total += c_zin[chunk, k].astype(F32)
        mine[...] = total
        last_out[chunk] = mine[given_rows, :]
        last[chunk] = send(last_out.at[chunk], last_in.at[chunk], at_tok(0, 0, 1))
        at = pl.multiple_of(core * (D // 2) + chunk * WIDE, 128)
        grad_head[:, pl.ds(at, WIDE)] = mine[kept_rows, :]

    plan = []
    for far, direct, joined, total, count, slot in (
        (far_y, direct_y, joined_y, total_y, CHUNKS, 1.55),
        (far_x, direct_x, joined_x, total_x, 6, 2.4),
    ):
        line = [(far, 0)]
        for n in range(count):
            if n + 1 < count:
                line.append((far, n + 1))
            line += [(direct, n), (joined, n)]
        for at, (step, n) in enumerate(line):
            plan.append((max(0, at + 1 - DEEP) * slot, step, n))
            if step is joined:
                plan.append(((at + 1) * slot + 2, total, n))
                if step is joined_y:
                    plan.append(((at + 1) * slot + 17, total_z, n))
    share.wait_recv()
    share_dlog.wait_recv()
    for _, step, n in sorted(plan, key=lambda entry: entry[0]):
        step(n)
    for chunk in range(CHUNKS):
        last[chunk].wait_recv()
        at = pl.multiple_of((1 - core) * (D // 2) + chunk * WIDE, 128)
        grad_head[:, pl.ds(at, WIDE)] = last_in[chunk]
    for copy in unsent.values():
        copy.wait_send()


def hand_over(*refs):
    for k in range(3):
        refs[3 + k][...] = refs[k][...]


COPIES = 42 + 2 + 7 + 6 * 6 + 6 + CHUNKS * 10


def per_device(hidden, head_weight, targets, loss_grad):
    vmem = pl.BlockSpec(memory_space=pltpu.VMEM)
    hbm = pl.BlockSpec(memory_space=pl.ANY)
    grad_in, grad_head, loss = pl.pallas_call(
        body,
        out_shape=(
            jax.ShapeDtypeStruct((COL, TOK), BF),
            jax.ShapeDtypeStruct((24, D), F32),
            jax.ShapeDtypeStruct((1, TOK), F32),
        ),
        in_specs=[hbm, hbm, vmem, vmem],
        out_specs=(vmem, vmem, vmem),
        scratch_shapes=[
            pltpu.VMEM((VOC, D), BF),
            pltpu.VMEM((D, VOC), BF),
            pltpu.VMEM((D, TOK), BF),
            pltpu.VMEM((D // 2, TOK), BF),
            pltpu.VMEM((VOC, TOK), F32),
            pltpu.VMEM((VOC, TOK), BF),
            pltpu.VMEM((VOC, TOK), BF),
            pltpu.VMEM((8, 8, TOK), F32),
            pltpu.VMEM((6, 6, PIECE, TOK), BF),
            pltpu.VMEM((6, 6, PIECE, TOK), BF),
            pltpu.VMEM((6, PIECE, TOK), BF),
            pltpu.VMEM((6, PIECE, TOK), BF),
            pltpu.VMEM((CHUNKS, 4, 4, GROUP, WIDE), F32),
            pltpu.VMEM((CHUNKS, 6, 2, GROUP, WIDE), BF),
            pltpu.VMEM((CHUNKS, 6, 2, GROUP, WIDE), BF),
            pltpu.VMEM((CHUNKS, 3, GROUP, WIDE), BF),
            pltpu.VMEM((CHUNKS, 3, GROUP, WIDE), BF),
            pltpu.VMEM((CHUNKS, 24, WIDE), F32),
            pltpu.VMEM((CHUNKS, 24, WIDE), F32),
            pltpu.SemaphoreType.DMA((2,)),
            pltpu.SemaphoreType.DMA((COPIES,)),
            pltpu.SemaphoreType.DMA((COPIES,)),
        ],
        compiler_params=pltpu.CompilerParams(
            collective_id=0, has_side_effects=True, vmem_limit_bytes=62 * 2**20
        ),
        name="head_backward",
    )(hidden.T, head_weight, targets.reshape(1, TOK), loss_grad.reshape(1, TOK))
    made = (grad_in, grad_head, loss)
    grad_in, grad_head, loss = pl.pallas_call(
        hand_over,
        out_shape=tuple(jax.ShapeDtypeStruct(a.shape, a.dtype) for a in made),
        in_specs=[vmem] * 3,
        out_specs=(vmem,) * 3,
        name="hand_over",
    )(*made)
    return grad_in.T, grad_head, loss.reshape(TOK)


def solution(mesh):
    in_specs = (P("tok", "vocab"), P("vocab", None), P("tok"), P("tok"))
    out_specs = (P("tok", "vocab"), P(("vocab", "tok"), None), P("tok"))
    return jax.shard_map(
        per_device, mesh=mesh, in_specs=in_specs, out_specs=out_specs, check_vma=False
    )
```

time: 140 us -> 116 us (0.83)
  Pallas kernels: 131 us -> 116 us
  local copies, waits for them, and re-layouts: 7.59 us -> 0 us
    pallas_call x1 -> x2, Pallas kernels: 131 us -> 116 us  [the longest x1 113 us: per_device(): pl.pallas_call(body, out_shape=(jax.ShapeDtypeStruct((COL, TOK), BF), jax...]
    unnamed x4 -> x0, local copies, waits for them, and re-layouts: 7.59 us -> none
where the time goes in v2:
time: 116 us
  Pallas kernels  116 us (100%)
    pallas_call x1, Pallas kernels, per_device(): pl.pallas_call(body, out_shape=(jax.ShapeDtypeStruct((COL, TOK), BF), jax...  113 us

profile of v2, /device:TPU:1, one launch (start us, length us, event | category | flops | bytes accessed | tf_op | source)
XLA Modules:
  0.0 116.2 jit_solution(8922723884312653757)
XLA Ops:
  0.6 113.2 %head_backward.1 = (bf16[672,512]{1,0:T(8,128)(2,1)}, f32[24,5376]{1,0:T(8,128)}, f32[1,512]{1,0:T(1,128)}) custom-call(bf16[672,512]{1,0:T(8,128)(2,1)} %bitcast.5, bf16[768,5376]{1,0:T(8,128)(2,1)} %weight.1, s32[1,512]{1,0:T(1,128)} %bitcast.6, f32[1,512]{1,0:T(1,128)} %bitcast.7), custom_call_target="tpu_custom_call" | custom-call | tf_op jit(solution)/shard_map/head_backward/pallas_call | solution.py:457
  113.8 2.3 %hand_over.1 = (bf16[672,512]{1,0:T(8,128)(2,1)}, f32[24,5376]{1,0:T(8,128)}, f32[1,512]{1,0:T(1,128)}) custom-call(bf16[672,512]{1,0:T(8,128)(2,1)} %get-tuple-element.9.refs_0_, f32[24,5376]{1,0:T(8,128)} %get-tuple-element.10.refs_1_, f32[1,512]{1,0:T(1,128)} %get-tuple-element.11.refs_2_), custom_call_target="tpu_custom_call" | custom-call | tf_op jit(solution)/shard_map/hand_over/pallas_call | solution.py:496

commit v3 on v2

v3 whole, which is shorter than its diff:
```python
import jax
import jax.numpy as jnp
from jax import lax
from jax.experimental import pallas as pl
from jax.experimental.pallas import tpu as pltpu
from jax.sharding import PartitionSpec as P

MESH = pl.DeviceIdType.MESH
D = 5376
VOC = 768
TOK = 512
COL = 672
PIECE = 112
CHUNKS = 7
HALVES = 1
PART = TOK // HALVES
ROWS = 112
LOWS = 336 // ROWS
GROUPS = 2 * HALVES * LOWS
DEEP = 3
RELAYED = 5
WIDE = D // 2 // CHUNKS
GROUP = 48
BF = jnp.bfloat16
F32 = jnp.float32


class Entry:
    def __init__(self, copy, at):
        self.copy, self.at = copy, at


def rows(start, size):
    return pl.ds(pl.multiple_of(start, 16), size)


def body(
    hidden, weight, targets, scales, grad_in, grad_head, loss,
    staged, weight_t, held, held_other, logits, dlog, dlog_other, stats,
    b_out, b_in, b_zout, b_zin, g_sum, c_out, c_in, c_zout, c_zin, last_out, last_in,
    local_sem, send_sem, recv_sem,
):
    vocab = lax.axis_index("vocab")
    tok = lax.axis_index("tok")
    x, z_lo = vocab // 2, vocab % 2
    core, y, z_hi = tok % 2, (tok // 2) % 4, tok // 8

    def in_vocab(dx, dz):
        return ((x + dx) % 4) * 2 + (z_lo + dz) % 2

    def in_tok(dz, dy, dc):
        return (((z_hi + dz + 4) % 4) * 4 + (y + dy) % 4) * 2 + (core + dc) % 2

    def at_vocab(dx, dz):
        return (in_vocab(dx, dz), tok)

    def at_tok(dz, dy, dc):
        return (vocab, in_tok(dz, dy, dc))

    peers = [at_vocab(dx, dz) for dx in range(4) for dz in range(2) if dx or dz]
    others = [at_tok(0, 0, 1), at_tok(0, 1, 0), at_tok(0, 3, 0)]
    others += [at_tok(dz, 0, 0) for dz in (1, 2, 3)]

    barrier = pltpu.get_barrier_semaphore()
    for device in peers + others:
        pl.semaphore_signal(barrier, inc=1, device_id=device, device_id_type=MESH)

    fetch_own = pltpu.make_async_copy(
        hidden, held.at[rows(vocab * COL, COL)], local_sem.at[0]
    )
    fetch_own.start()
    fetch = pltpu.make_async_copy(weight, staged, local_sem.at[1])
    fetch.start()

    spare, used, unsent, lanes = [], [0, 0], [], {}

    def new_arrival():
        used[1] += 1
        return used[1] - 1

    def sent(entry):
        entry.copy.wait_send()
        unsent.remove(entry)
        spare.append(entry.at)

    def send(src, dst, device, into, lane, most):
        queue = lanes.setdefault(lane, [])
        while len(queue) >= most:
            sent(queue.pop(0))
        if not spare:
            spare.append(used[0])
            used[0] += 1
        at = spare.pop()
        copy = pltpu.make_async_remote_copy(
            src_ref=src,
            dst_ref=dst,
            send_sem=send_sem.at[at],
            recv_sem=recv_sem.at[into],
            device_id=device,
            device_id_type=MESH,
        )
        copy.start()
        entry = Entry(copy, at)
        queue.append(entry)
        unsent.append(entry)

    def arrive(ref, at):
        pltpu.make_async_remote_copy(
            src_ref=ref,
            dst_ref=ref,
            send_sem=send_sem.at[0],
            recv_sem=recv_sem.at[at],
            device_id=at_tok(0, 0, 1),
            device_id_type=MESH,
        ).wait_recv()

    right, left, pair = at_vocab(1, 0), at_vocab(3, 0), at_vocab(0, 1)
    own = vocab
    from_left, from_right = in_vocab(3, 0), in_vocab(1, 0)
    across, partner = in_vocab(2, 0), in_vocab(0, 1)

    arrival, ready = {}, set()
    source = {
        "left": from_left,
        "right": from_right,
        "pair": partner,
        "across": across,
        "pair left": in_vocab(3, 1),
        "pair right": in_vocab(1, 1),
        "pair across": in_vocab(2, 1),
    }

    def lanes_of(half):
        return pl.ds(half * PART, PART)

    def spot(block, part, half):
        return held.at[rows(block * COL + part * PIECE, PIECE), lanes_of(half)]

    def together(key):
        return key.startswith("pair ")

    def need(key, part, half):
        if together(key):
            part = 0
        if (key, part, half) not in ready:
            ready.add((key, part, half))
            ref = spot(source[key], part, half)
            if together(key):
                ref = held.at[rows(source[key] * COL, COL), lanes_of(half)]
            arrive(ref, arrival[key, part, half])

    def pass_on(block, part, half, device, lane, key):
        name = key, 0 if together(key) else part, half
        if name not in arrival:
            arrival[name] = new_arrival()
        where = spot(block, part, half)
        send(where, where, device, arrival[name], lane, HALVES + 1)

    def own_right(part, half):
        pass_on(own, part, half, right, "right", "left")

    def own_left(part, half):
        pass_on(own, part, half, left, "left", "right")

    def own_pair(part, half):
        pass_on(own, part, half, pair, "pair", "pair")

    def on_right(part, half):
        need("left", part, half)
        pass_on(from_left, part, half, right, "right", "across")

    def on_left(part, half):
        need("right", part, half)
        pass_on(from_right, part, half, left, "left", "across")

    def z_right(part, half):
        need("pair", part, half)
        pass_on(partner, part, half, right, "right", "pair left")

    def z_left(part, half):
        need("pair", part, half)
        pass_on(partner, part, half, left, "left", "pair right")

    def pair_from_right(part, half):
        need("right", part, half)
        pass_on(from_right, part, half, pair, "pair", "pair right")

    def pair_from_left(part, half):
        need("left", part, half)
        pass_on(from_left, part, half, pair, "pair", "pair left")

    def pair_across(part, half):
        need("across", part, half)
        pass_on(across, part, half, pair, "pair", "pair across")

    fetch_own.wait()
    pl.semaphore_wait(barrier, len(peers) + len(others))

    def turn(first, count):
        def step(i, _):
            at = pl.multiple_of((first + i) * 128, 128)
            weight_t[pl.ds(at, 128), :] = staged[:, pl.ds(at, 128)].T
            return 0

        lax.fori_loop(0, count, step, 0)

    def logit_range(start, size, half, fresh=False):
        tokens = lanes_of(half)
        start = pl.multiple_of(start, 128)

        def step(i, _):
            at = pl.multiple_of(i * 384, 384)
            part = jnp.dot(
                staged[pl.ds(at, 384), pl.ds(start, size)],
                held[pl.ds(start, size), tokens],
                preferred_element_type=F32,
            )
            if fresh:
                logits[pl.ds(at, 384), tokens] = part
            else:
                logits[pl.ds(at, 384), tokens] += part
            return 0

        lax.fori_loop(0, VOC // 384, step, 0)

    def logit_part(block, half, fresh=False):
        quad, rest = block // 4, block % 4
        logit_range(quad * 2688 + rest * 704 + (rest % 2) * 64, 512, half, fresh)

    def logit_rest(half):
        for start, size in ((512, 256), (1280, 128), (1920, 256)):
            logit_range(start, size, half)
            logit_range(2688 + start, size, half)

    def whole(key, block, half):
        for part in range(6):
            need(key, part, half)
        logit_part(block, half)

    shares = []

    def give_share(half):
        shares.append((held_other.at[:, lanes_of(half)], new_arrival()))
        mine = held.at[rows((1 - core) * (D // 2), D // 2), lanes_of(half)]
        send(mine, *shares[-1][:1], at_tok(0, 0, 1), shares[-1][1], "core", 2)

    steps = VOC // 64
    ids = lax.broadcasted_iota(jnp.int32, (64, PART), 0)
    zeros = jnp.zeros((8, PART), F32)
    peak_of, chosen_of, told_of = {}, {}, {}

    def local_softmax(half):
        tokens = lanes_of(half)
        chosen = targets[:, tokens] - vocab * VOC

        def find_peak(i, peak):
            part = logits[pl.ds(pl.multiple_of(i * 64, 64), 64), tokens]
            return jnp.maximum(peak, jnp.max(part.reshape(8, 8, PART), axis=0))

        peak = jnp.full((8, PART), -jnp.inf, F32)
        peak = lax.fori_loop(0, steps, find_peak, peak)
        peak = jnp.max(peak, axis=0, keepdims=True)

        def add_up(i, carry):
            total, picked = carry
            at = pl.multiple_of(i * 64, 64)
            part = logits[pl.ds(at, 64), tokens]
            hit = ids == chosen - at
            picked += jnp.sum(jnp.where(hit, part, 0.0).reshape(8, 8, PART), axis=0)
            part = jnp.exp(part - peak)
            logits[pl.ds(at, 64), tokens] = part
            total += jnp.sum(part.reshape(8, 8, PART), axis=0)
            return total, picked

        total, picked = lax.fori_loop(0, steps, add_up, (zeros, zeros))
        total = jnp.sum(total, axis=0, keepdims=True)
        picked = jnp.sum(picked, axis=0, keepdims=True)
        stats[half, own] = jnp.concatenate([peak, total, picked, zeros[:5]], axis=0)
        where = stats.at[half, own]
        told_of[half] = new_arrival()
        for device in peers:
            send(where, where, device, told_of[half], "stats", 7)
        peak_of[half], chosen_of[half] = peak, chosen

    def full_softmax(half):
        tokens = lanes_of(half)
        arrive(stats.at[half, pl.ds(0, 7)], told_of[half])
        heard = stats[half]
        peaks, totals, picks = heard[:, 0, :], heard[:, 1, :], heard[:, 2, :]
        row_peak = jnp.max(peaks, axis=0, keepdims=True)
        row_total = jnp.sum(totals * jnp.exp(peaks - row_peak), axis=0, keepdims=True)
        target_logit = jnp.sum(picks, axis=0, keepdims=True)
        loss[:, tokens] = row_peak + jnp.log(row_total) - target_logit
        share_of = jnp.exp(peak_of[half] - row_peak) / row_total
        scale, chosen = scales[:, tokens], chosen_of[half]

        def make_dlog(i, _):
            at = pl.multiple_of(i * 64, 64)
            part = logits[pl.ds(at, 64), tokens] * share_of
            hit = ids == chosen - at
            part = scale * (part - jnp.where(hit, 1.0, 0.0))
            dlog[pl.ds(at, 64), tokens] = part.astype(BF)
            return 0

        lax.fori_loop(0, steps, make_dlog, 0)
        shares.append((dlog_other.at[:, tokens], new_arrival()))
        send(dlog.at[:, tokens], *shares[-1][:1], at_tok(0, 0, 1), shares[-1][1], "core", 2)

    order_right = [(own_right, p) for p in (0, 1, 2)]
    order_right += [(on_right, 0), (own_right, 3), (on_right, 1), (own_right, 4)]
    order_right += [(on_right, 2), (own_right, 5)] + [(z_right, p) for p in range(5)]
    order_left = [(own_left, p) for p in (5, 4, 3)]
    order_left += [(on_left, 5), (own_left, 2), (on_left, 4), (own_left, 1)]
    order_left += [(on_left, 3), (own_left, 0)] + [(z_left, p) for p in range(5)]
    order_pair = [(own_pair, p) for p in range(6)]
    order_pair += [(pair_from_right, 5), (pair_across, 0), (pair_across, 5)]
    order_pair += [(pair_across, 1), (pair_across, 4), (pair_from_left, 5)]
    order_pair += [(pair_across, 2), (pair_across, 3)]

    def work(slot, half):
        if slot == 1 and half == 0:
            fetch.wait()
        if 1 <= slot <= 7 and half == 0:
            turn(6 * slot - 6, 6)
        if slot == 8:
            logit_part(own, half, fresh=True)
        if slot == 10:
            whole("pair", partner, half)
        if slot == 12:
            whole("left", from_left, half)
        if slot == 13:
            whole("right", from_right, half)
        if slot == 14:
            whole("across", across, half)
        if slot == 16:
            whole("pair left", in_vocab(3, 1), half)
        if slot == 17:
            whole("pair right", in_vocab(1, 1), half)
        if slot == 18:
            whole("pair across", in_vocab(2, 1), half)
            give_share(half)
            logit_rest(half)
        if slot == 19:
            local_softmax(half)
        if slot == 23:
            full_softmax(half)

    for slot in range(14 * HALVES):
        for order in (order_right, order_left, order_pair):
            step, part = order[slot % 14]
            step(part, slot // 14)
        for half in range(HALVES):
            work(slot - 14 * half, half)

    def input_part(block, part, half):
        return jnp.dot(
            weight_t[rows(block * COL + part * ROWS, ROWS), :],
            dlog[:, lanes_of(half)],
            preferred_element_type=F32,
        )

    def to_x(device, lane, group, slot, part):
        b_out[group, slot] = part.astype(BF)
        where = b_out.at[group, slot], b_in.at[group, slot]
        send(*where, device, arrive_b[group][slot // 2 > 0], lane, DEEP)

    def to_left(group, slot, part):
        to_x(left, "left", group, slot, part)

    def to_right(group, slot, part):
        to_x(right, "right", group, slot, part)

    def arrived(group, slot):
        return b_in[group, slot].astype(F32)

    arrive_b, plane_b = {}, {}

    def place(group):
        half, rest = group // (2 * LOWS), group % (2 * LOWS)
        return half, 1 - rest // LOWS, rest % LOWS

    def far_x(group):
        arrive_b[group] = new_arrival(), new_arrival()
        half, plane, low = place(group)
        block = in_vocab(2, plane)
        to_left(group, 0, input_part(block, low, half))
        to_right(group, 1, input_part(block, low + LOWS, half))

    def direct_x(group):
        half, plane, low = place(group)
        to_left(group, 2, input_part(in_vocab(3, plane), low + LOWS, half))
        to_right(group, 3, input_part(in_vocab(1, plane), low, half))

    def joined_x(group):
        half, plane, low = place(group)
        a = input_part(in_vocab(3, plane), low, half)
        b = input_part(in_vocab(1, plane), low + LOWS, half)
        arrive(b_in.at[group, pl.ds(0, 2)], arrive_b[group][0])
        to_left(group, 4, a + arrived(group, 0))
        to_right(group, 5, b + arrived(group, 1))

    def total_x(group):
        half, plane, low = place(group)
        block = in_vocab(0, plane)
        a = input_part(block, low, half)
        b = input_part(block, low + LOWS, half)
        arrive(b_in.at[group, pl.ds(2, 4)], arrive_b[group][1])
        a += arrived(group, 3) + arrived(group, 4)
        b += arrived(group, 2) + arrived(group, 5)
        if plane:
            plane_b[half, low] = new_arrival()
            for k, part in enumerate((a, b)):
                b_zout[half, low, k] = part.astype(BF)
                where = b_zout.at[half, low, k], b_zin.at[half, low, k]
                send(*where, pair, plane_b[half, low], "pair", 4)
        else:
            tokens = lanes_of(half)
            arrive(b_zin.at[half, low], plane_b[half, low])
            a += b_zin[half, low, 0].astype(F32)
            grad_in[pl.ds(low * ROWS, ROWS), tokens] = a.astype(BF)
            b += b_zin[half, low, 1].astype(F32)
            grad_in[pl.ds((low + LOWS) * ROWS, ROWS), tokens] = b.astype(BF)

    up, down = at_tok(0, 1, 0), at_tok(0, 3, 0)

    def head_part(chunk):
        def step(i, _):
            two = pl.multiple_of(i * 768, 768)
            for mine, kept, first in (
                (dlog, held, core * (D // 2)),
                (dlog_other, held_other, 0),
            ):
                part = lax.dot_general(
                    mine[pl.ds(two, 768), :],
                    kept[rows(first + chunk * WIDE, WIDE), :],
                    (((1,), (1,)), ((), ())),
                    preferred_element_type=F32,
                ).reshape(4, 4, GROUP, WIDE)
                if kept is held:
                    g_sum[chunk] = part
                else:
                    g_sum[chunk] += part
            return 0

        lax.fori_loop(0, 1, step, 0)

    def to_y(device, lane, chunk, slot, part):
        c_out[chunk, slot] = part.astype(BF)
        where = c_out.at[chunk, slot], c_in.at[chunk, slot]
        send(*where, device, arrive_c[chunk][slot // 2 > 0], lane, DEEP)

    def to_down(chunk, slot, part):
        to_y(down, "down", chunk, slot, part)

    def to_up(chunk, slot, part):
        to_y(up, "up", chunk, slot, part)

    def landed(chunk, slot):
        return c_in[chunk, slot].astype(F32)

    arrive_c, arrive_z, arrive_last = {}, {}, new_arrival()
    low, high = pl.ds(0, 2), pl.ds(2, 2)

    def far_y(chunk):
        arrive_c[chunk] = new_arrival(), new_arrival()
        if chunk == 0:
            for shared in shares:
                arrive(*shared)
        head_part(chunk)
        to = (y + 2) % 4
        to_down(chunk, 0, g_sum[chunk, low, to])
        to_up(chunk, 1, g_sum[chunk, high, to])

    def direct_y(chunk):
        to_down(chunk, 2, g_sum[chunk, high, (y + 3) % 4])
        to_up(chunk, 3, g_sum[chunk, low, (y + 1) % 4])

    def joined_y(chunk):
        arrive(c_in.at[chunk, pl.ds(0, 2)], arrive_c[chunk][0])
        to_down(chunk, 4, g_sum[chunk, low, (y + 3) % 4] + landed(chunk, 0))
        to_up(chunk, 5, g_sum[chunk, high, (y + 1) % 4] + landed(chunk, 1))

    def total_y(chunk):
        arrive(c_in.at[chunk, pl.ds(2, 4)], arrive_c[chunk][1])
        g_sum[chunk, low, y] += landed(chunk, 3) + landed(chunk, 4)
        g_sum[chunk, high, y] += landed(chunk, 2) + landed(chunk, 5)
        arrive_z[chunk] = new_arrival(), new_arrival()
        turn_z = 1 - 2 * (chunk % 2)
        to_z(chunk, 0, turn_z * (1 + (chunk >= RELAYED)), g_sum[chunk, (z_hi + 2) % 4, y])
        to_z(chunk, 1, -turn_z, g_sum[chunk, (z_hi - turn_z + 4) % 4, y])
        if chunk >= RELAYED:
            to_z(chunk, 2, turn_z, g_sum[chunk, (z_hi + turn_z + 4) % 4, y])

    def to_z(chunk, slot, by, part):
        c_zout[chunk, slot] = part.astype(BF)
        where = c_zout.at[chunk, slot], c_zin.at[chunk, slot]
        send(*where, at_tok(by, 0, 0), arrive_z[chunk][slot > 0], "z", 9)

    def joined_z(chunk):
        if chunk >= RELAYED:
            return
        turn_z = 1 - 2 * (chunk % 2)
        arrive(c_zin.at[chunk, 0], arrive_z[chunk][0])
        part = g_sum[chunk, (z_hi + turn_z + 4) % 4, y]
        to_z(chunk, 2, turn_z, part + c_zin[chunk, 0].astype(F32))

    kept_rows = pl.ds(pl.multiple_of(core * 24, 8), 24)
    given_rows = pl.ds(pl.multiple_of((1 - core) * 24, 8), 24)

    def total_z(chunk):
        if chunk >= RELAYED:
            arrive(c_zin.at[chunk, 0], arrive_z[chunk][0])
        arrive(c_zin.at[chunk, pl.ds(1, 2)], arrive_z[chunk][1])
        mine = g_sum.at[chunk, z_hi, y]
        total = mine[...] + c_zin[chunk, 1].astype(F32) + c_zin[chunk, 2].astype(F32)
        if chunk >= RELAYED:
            total += c_zin[chunk, 0].astype(F32)
        mine[...] = total
        last_out[chunk] = mine[given_rows, :]
        where = last_out.at[chunk], last_in.at[chunk]
        send(*where, at_tok(0, 0, 1), arrive_last, "core", 8)
        at = pl.multiple_of(core * (D // 2) + chunk * WIDE, 128)
        grad_head[:, pl.ds(at, WIDE)] = mine[kept_rows, :]

    plan = []
    for slot in range(14, 24):
        work(slot, HALVES - 1)
    for far, direct, joined, total, count, slot in (
        (far_x, direct_x, joined_x, total_x, GROUPS, 14.5 / GROUPS),
        (far_y, direct_y, joined_y, total_y, CHUNKS, 1.55),
    ):
        line = [(far, 0), (direct, 0)]
        for n in range(count):
            if n + 1 < count:
                line += [(far, n + 1), (joined, n), (direct, n + 1)]
            else:
                line.append((joined, n))
        for at, (step, n) in enumerate(line):
            plan.append((max(at * 0.01, (at + 1 - DEEP) * slot), step, n))
            if step is joined:
                plan.append(((at + 1) * slot + 2, total, n))
                if step is joined_y:
                    plan.append(((at + 1) * slot + 6, joined_z, n))
                    plan.append(((at + 1) * slot + 17, total_z, n))
    for _, step, n in sorted(plan, key=lambda entry: entry[0]):
        step(n)
    arrive(last_in, arrive_last)
    for chunk in range(CHUNKS):
        at = pl.multiple_of((1 - core) * (D // 2) + chunk * WIDE, 128)
        grad_head[:, pl.ds(at, WIDE)] = last_in[chunk]
    for entry in list(unsent):
        sent(entry)
    assert used[0] <= SENDS and used[1] <= ARRIVALS


def hand_over(*refs):
    for k in range(3):
        refs[3 + k][...] = refs[k][...]


SENDS, ARRIVALS = 40, 74


def per_device(hidden, head_weight, targets, loss_grad):
    vmem = pl.BlockSpec(memory_space=pltpu.VMEM)
    hbm = pl.BlockSpec(memory_space=pl.ANY)
    grad_in, grad_head, loss = pl.pallas_call(
        body,
        out_shape=(
            jax.ShapeDtypeStruct((COL, TOK), BF),
            jax.ShapeDtypeStruct((24, D), F32),
            jax.ShapeDtypeStruct((1, TOK), F32),
        ),
        in_specs=[hbm, hbm, vmem, vmem],
        out_specs=(vmem, vmem, vmem),
        scratch_shapes=[
            pltpu.VMEM((VOC, D), BF),
            pltpu.VMEM((D, VOC), BF),
            pltpu.VMEM((D, TOK), BF),
            pltpu.VMEM((D // 2, TOK), BF),
            pltpu.VMEM((VOC, TOK), F32),
            pltpu.VMEM((VOC, TOK), BF),
            pltpu.VMEM((VOC, TOK), BF),
            pltpu.VMEM((HALVES, 8, 8, PART), F32),
            pltpu.VMEM((GROUPS, 6, ROWS, PART), BF),
            pltpu.VMEM((GROUPS, 6, ROWS, PART), BF),
            pltpu.VMEM((HALVES, LOWS, 2, ROWS, PART), BF),
            pltpu.VMEM((HALVES, LOWS, 2, ROWS, PART), BF),
            pltpu.VMEM((CHUNKS, 4, 4, GROUP, WIDE), F32),
            pltpu.VMEM((CHUNKS, 6, 2, GROUP, WIDE), BF),
            pltpu.VMEM((CHUNKS, 6, 2, GROUP, WIDE), BF),
            pltpu.VMEM((CHUNKS, 3, GROUP, WIDE), BF),
            pltpu.VMEM((CHUNKS, 3, GROUP, WIDE), BF),
            pltpu.VMEM((CHUNKS, 24, WIDE), F32),
            pltpu.VMEM((CHUNKS, 24, WIDE), F32),
            pltpu.SemaphoreType.DMA((2,)),
            pltpu.SemaphoreType.DMA((SENDS,)),
            pltpu.SemaphoreType.DMA((ARRIVALS,)),
        ],
        compiler_params=pltpu.CompilerParams(
            collective_id=0, has_side_effects=True, vmem_limit_bytes=62 * 2**20
        ),
        name="head_backward",
    )(hidden.T, head_weight, targets.reshape(1, TOK), loss_grad.reshape(1, TOK))
    made = (grad_in, grad_head, loss)
    grad_in, grad_head, loss = pl.pallas_call(
        hand_over,
        out_shape=tuple(jax.ShapeDtypeStruct(a.shape, a.dtype) for a in made),
        in_specs=[vmem] * 3,
        out_specs=(vmem,) * 3,
        name="hand_over",
    )(*made)
    return grad_in.T, grad_head, loss.reshape(TOK)


def solution(mesh):
    in_specs = (P("tok", "vocab"), P("vocab", None), P("tok"), P("tok"))
    out_specs = (P("tok", "vocab"), P(("vocab", "tok"), None), P("tok"))
    return jax.shard_map(
        per_device, mesh=mesh, in_specs=in_specs, out_specs=out_specs, check_vma=False
    )
```

time: 116 us -> 116 us (level)
  no operation moved by 1% of the time
where the time goes in v3:
time: 116 us
  Pallas kernels  115 us (99%)
    pallas_call x1, Pallas kernels, per_device(): pl.pallas_call(body, out_shape=(jax.ShapeDtypeStruct((COL, TOK), BF), jax...  113 us

profile of v3, /device:TPU:1, one launch (start us, length us, event | category | flops | bytes accessed | tf_op | source)
XLA Modules:
  0.0 116.1 jit_solution(13695444864219577665)
XLA Ops:
  0.6 113.1 %head_backward.1 = (bf16[672,512]{1,0:T(8,128)(2,1)}, f32[24,5376]{1,0:T(8,128)}, f32[1,512]{1,0:T(1,128)}) custom-call(bf16[672,512]{1,0:T(8,128)(2,1)} %bitcast.5, bf16[768,5376]{1,0:T(8,128)(2,1)} %weight.1, s32[1,512]{1,0:T(1,128)} %bitcast.6, f32[1,512]{1,0:T(1,128)} %bitcast.7), custom_call_target="tpu_custom_call" | custom-call | tf_op jit(solution)/shard_map/head_backward/pallas_call | solution.py:567
  113.8 2.3 %hand_over.1 = (bf16[672,512]{1,0:T(8,128)(2,1)}, f32[24,5376]{1,0:T(8,128)}, f32[1,512]{1,0:T(1,128)}) custom-call(bf16[672,512]{1,0:T(8,128)(2,1)} %get-tuple-element.9.refs_0_, f32[24,5376]{1,0:T(8,128)} %get-tuple-element.10.refs_1_, f32[1,512]{1,0:T(1,128)} %get-tuple-element.11.refs_2_), custom_call_target="tpu_custom_call" | custom-call | tf_op jit(solution)/shard_map/hand_over/pallas_call | solution.py:606
